TPU v7x, 32 devices: a whole 2x2x4 slice. The times are simulated.
32 devices in a mesh: det: 8 (over z, x), tm: 4 (over y, core).
Axes of the slice: x: 2, y: 2, z: 4, core: 2. Of those that a mesh axis runs over, the one named last changes fastest.
Arguments:
- x_map: float32 [3, 4096, 256], P(None, ('det', 'tm')), may hold values from -6 to 6
- r_map: float32 [3, 4096, 256], P(None, ('det', 'tm')), may hold values from -45 to 45
- p_map: float32 [3, 4096, 256], P(None, ('det', 'tm')), may hold values from -45 to 45
- pointing: int32 [32, 16384], P('det', 'tm'), may hold values from 0 to 2047
- pol_angle: float32 [32, 16384], P('det', 'tm'), may hold values from -3.140625 to 3.140625
- noise_filter: bfloat16 [32, 8192], P('det'), may hold values from -2 to 2
- block_list: int32 [8, 128, 8], P('det', 'tm'), may hold values from 0 to 4095, as said below
- block_home: int32 [4096], replicated, may hold values from 0 to 4095, as said below
Outputs:
- x_next: float32 [3, 4096, 256], P(None, ('det', 'tm'))
- r_next: float32 [3, 4096, 256], P(None, ('det', 'tm'))
- p_next: float32 [3, 4096, 256], P(None, ('det', 'tm'))
Inputs may be any that keep to these rules, and one draw needn't show every extreme that they name: Block b is stored at row block_home[b] of the maps, a permutation. `block_list`: repeats allowed. The 256 entries of one device's lists name at most 16 blocks stored on any one device (counted with repeats), exactly 16 on some; one device's stored blocks are named 16 times by every device's lists.
All inputs are finite; a program needn't handle non-finite values.
Results may differ from a plain program's by a relative error of at most 0.0034.
The roundings to bfloat16 on the way count: a program that leaves them out, or rounds other values in their place, can miss the bound.
Values may be sent and summed in bfloat16 or wider, within the bound.
A program may use at most 128 MiB of HBM per device.

v0:
```python
import jax
import jax.numpy as jnp
from jax import lax
from jax.sharding import PartitionSpec as P


def with_halo(block, sides, width):
    for axis, dim in sides:
        count = lax.axis_size(axis)
        forward = [(i, i + 1) for i in range(count - 1)]
        backward = [(target, source) for source, target in forward]
        low = lax.ppermute(
            lax.slice_in_dim(block, block.shape[dim] - width, None, axis=dim), axis, forward
        )
        high = lax.ppermute(lax.slice_in_dim(block, 0, width, axis=dim), axis, backward)
        block = jnp.concatenate([low, block, high], axis=dim)
    return block


def apply_filter(padded, noise_filter, samples):
    tap_count = noise_filter.shape[1]
    window_len = tap_count + 128
    windows = samples // 128
    span_rows = tap_count // 128 + 1

    def one_detector(series, coeffs):
        extended = jnp.concatenate([coeffs, jnp.zeros((129,), coeffs.dtype)])
        toeplitz = jnp.tile(extended, 128)[: 128 * window_len].reshape(128, window_len)
        pieces = series.reshape(-1, 128)
        framed = jnp.stack(
            [pieces[offset_rows : offset_rows + windows] for offset_rows in range(span_rows)],
            axis=1,
        )
        framed = framed.reshape(windows, window_len)
        result = lax.dot_general(
            framed, toeplitz, (((1,), (1,)), ((), ())), preferred_element_type=jnp.float32
        )
        return result.reshape(samples)

    groups = padded.shape[0] // 4

    def one_group(bundle):
        return jax.vmap(one_detector)(bundle[0], bundle[1])

    output = lax.map(
        one_group, (padded.reshape(groups, 4, -1), noise_filter.reshape(groups, 4, tap_count))
    )
    return output.reshape(-1, samples)


def body(x_map, r_map, p_map, pointing, pol_angle, noise_filter, block_list, block_home):
    det_count = lax.axis_size("det")
    time_count = lax.axis_size("tm")
    devices = det_count * time_count
    list_len = block_list.shape[2]
    per_device = block_list.shape[1] * list_len
    capacity = 2 * per_device // devices
    slot_count = devices * capacity
    blocks_here = p_map.shape[1]
    pixels = p_map.shape[2]
    wanted = block_list.reshape(per_device)
    stored = jnp.take(block_home, wanted)
    owner_index = stored // blocks_here
    slot_of = stored % blocks_here
    member = (owner_index[:, None] == jnp.arange(devices, dtype=jnp.int32)[None, :]).astype(
        jnp.int32
    )
    ranking = jnp.sum((jnp.cumsum(member, axis=0) - 1) * member, axis=1)
    send_place = owner_index * capacity + ranking
    request = jnp.full((slot_count,), -1, jnp.int32).at[send_place].set(slot_of)
    asked_slots = lax.all_to_all(request, ("det", "tm"), split_axis=0, concat_axis=0, tiled=True)
    present = asked_slots >= 0
    answer = jnp.where(present[None, :, None], p_map[:, jnp.maximum(asked_slots, 0), :], 0.0)
    fetched = lax.all_to_all(answer, ("det", "tm"), split_axis=1, concat_axis=1, tiled=True)
    local_map = fetched[:, send_place, :].reshape(3, per_device * pixels)
    samples = pointing.shape[1]
    block_span = samples // block_list.shape[1]
    time_block = jnp.arange(samples, dtype=jnp.int32) // block_span
    address = time_block[None, :] * (list_len * pixels) + pointing
    cosine = jnp.cos(2.0 * pol_angle)
    sine_part = jnp.sin(2.0 * pol_angle)
    signal = (
        local_map[0][address] + cosine * local_map[1][address] + sine_part * local_map[2][address]
    ).astype(jnp.bfloat16)
    tap_count = noise_filter.shape[1]
    padded = with_halo(signal, (("tm", 1),), tap_count // 2)
    rounded = apply_filter(padded, noise_filter, samples).astype(jnp.bfloat16)
    filtered = lax.optimization_barrier(rounded).astype(jnp.float32)
    terms = jnp.stack([filtered, filtered * cosine, filtered * sine_part]).reshape(3, -1)
    partial_value = (
        jnp.zeros((3, per_device * pixels), jnp.float32).at[:, address.reshape(-1)].add(terms)
    )
    outgoing = (
        jnp.zeros((3, slot_count, pixels), jnp.float32)
        .at[:, send_place, :]
        .set(partial_value.reshape(3, per_device, pixels))
    )
    returned = lax.all_to_all(outgoing, ("det", "tm"), split_axis=1, concat_axis=1, tiled=True)
    selector = (asked_slots[:, None] == jnp.arange(blocks_here, dtype=jnp.int32)[None, :]).astype(
        jnp.float32
    )
    image = jnp.einsum("sk,csb->ckb", selector, returned, precision=lax.Precision.HIGHEST)
    norm_old = lax.psum(jnp.sum(r_map * r_map), ("det", "tm"))
    curvature = lax.psum(jnp.sum(p_map * image), ("det", "tm"))
    step_size = norm_old / curvature
    r_next = r_map - step_size * image
    norm_new = lax.psum(jnp.sum(r_next * r_next), ("det", "tm"))
    x_next = x_map + step_size * p_map
    p_next = r_next + norm_new / norm_old * p_map
    return (x_next, r_next, p_next)


def solution(mesh):
    return jax.shard_map(
        body,
        mesh=mesh,
        in_specs=(
            P(None, ("det", "tm"), None),
            P(None, ("det", "tm"), None),
            P(None, ("det", "tm"), None),
            P("det", "tm"),
            P("det", "tm"),
            P("det", None),
            P("det", "tm", None),
            P(),
        ),
        out_specs=(
            P(None, ("det", "tm"), None),
            P(None, ("det", "tm"), None),
            P(None, ("det", "tm"), None),
        ),
        check_vma=False,
    )
```

profile of v0, /device:TPU:0, one launch (start us, length us, event | category | flops | bytes accessed | tf_op | source)
XLA Modules:
  0.0 697.4 jit_solution(10474817990767673283)
XLA Ops:
  6.0 14.2 %all_to_all.22 = s32[32,16,1]{1,2,0:T(1,128)S(1)} all-to-all(s32[32,16,1]{1,2,0:T(1,128)S(1)} %bitcast.432), channel_id=1, replica_groups=mesh['det'=8,'tm'=4] {'det','tm'}, dimensions={0} | all-to-all | bytes 4096 | tf_op jit(solution)/shard_map/all_to_all | solution.py:71
  22.2 3.7 gather_fusion.1
  26.0 2.4 copy.112
  28.5 2.9 all-to-all-start.1
  32.8 47.3 %all-to-all-done.1 = f32[3,512,256]{2,0,1:T(4,128)S(1)} async-done(((f32[3,512,256]{2,0,1:T(4,128)}), f32[3,512,256]{2,0,1:T(4,128)S(1)}, u32[]{:S(2)}, u32[]{:S(2)}) %all-to-all-start.1) | async-done | bytes 1572896 | tf_op jit(solution)/shard_map/all_to_all | solution.py:74
  81.9 90.8 %gather_fusion.3 = f32[16384]{0:T(1024)S(1)} fusion(f32[65536]{0:T(1024)S(1)} %bitcast.354, s32[16384]{0:T(1024)} %broadcast_clamp_fusion), kind=kCustom, calls=%fused_computation.3 | custom fusion | bytes 196608 | tf_op jit(solution)/shard_map/gather | solution.py:83
  172.8 90.5 %gather_fusion.4 = f32[16384]{0:T(1024)S(1)} fusion(f32[65536]{0:T(1024)S(1)} %bitcast.353, s32[16384]{0:T(1024)S(1)} %copy-done.5), kind=kCustom, calls=%fused_computation.4 | custom fusion | bytes 196608 | tf_op jit(solution)/shard_map/gather | solution.py:83
  263.4 90.5 %gather_fusion.5 = f32[16384]{0:T(1024)S(1)} fusion(f32[65536]{0:T(1024)S(1)} %bitcast.352, s32[16384]{0:T(1024)S(1)} %copy-done.5), kind=kCustom, calls=%fused_computation.5 | custom fusion | bytes 196608 | tf_op jit(solution)/shard_map/gather | solution.py:83
  357.9 3.9 tile.14
  361.8 18.0 %reshape.389 = bf16[4260352]{0:T(1024)(128)(2,1)} reshape(bf16[4,128,8321]{2,1,0:T(8,128)(2,1)} %tile.14) | data formatting | bytes 17041408
  379.7 15.0 %tile.15 = bf16[4,1065088]{1,0:T(4,128)(2,1)} reshape(bf16[4260352]{0:T(1024)(128)(2,1)} %reshape.389) | data formatting | bytes 17041408 | tf_op jit(solution)/shard_map/while/body/eval_jaxpr/vmap()/tile | solution.py:28
  396.2 1.9 slice-done
  398.1 3.0 fusion.17
  402.1 5.2 copy.114
  407.3 100.8 %scatter_custom_fusion.1 = f32[3,65536]{0,1:T(8,128)} fusion(s32[16384]{0:T(1024)S(1)} %bitcast.431, f32[16384,3]{1,0:T(8,128)} %copy.114, f32[]{:T(128)} %constant.81.clone.1), kind=kCustom, calls=%fused_computation.9 | custom fusion | flops 49152 | bytes 786944 | tf_op jit(solution)/shard_map/scatter-add | solution.py:91
  508.1 17.9 %copy.115 = f32[3,256,256]{2,0,1:T(4,128)S(1)} copy(f32[3,256,256]{0,2,1:T(8,128)} %bitcast.355) | data formatting | bytes 1572864 | tf_op jit(solution)/shard_map/reshape | solution.py:96
  527.7 24.0 %scatter_fusion = f32[3,512,256]{2,0,1:T(4,128)} fusion(f32[3,512,256]{2,0,1:T(4,128)} %broadcast_in_dim.31, s32[256]{0:T(256)S(1)} %bitcast.436, f32[256,3,256]{2,1,0:T(4,128)S(1)} %bitcast.422), kind=kCustom, calls=%fused_computation.8 | custom fusion | bytes 2360320 | tf_op jit(solution)/shard_map/scatter | solution.py:96
  551.6 6.7 all-to-all-start.2
  559.4 1.9 copy.119
  562.0 45.1 %all-to-all-done.2 = f32[3,512,256]{2,0,1:T(4,128)S(1)} async-done(((f32[3,512,256]{2,0,1:T(4,128)}), f32[3,512,256]{2,0,1:T(4,128)S(1)}, u32[]{:S(2)}, u32[]{:S(2)}) %all-to-all-start.2) | async-done | bytes 1572896 | tf_op jit(solution)/shard_map/all_to_all | solution.py:98
  607.1 2.9 multiply_reduce_fusion.1
  610.0 38.4 %all-reduce.1 = (f32[]{:T(128)}, f32[]{:T(128)}) all-reduce(f32[]{:T(128)} %multiply_reduce_fusion.2, f32[]{:T(128)} %get-tuple-element.41), channel_id=1, replica_groups=mesh['det'=8,'tm'=4] {'det','tm'}, use_global_device_ids=true, to_apply=%region_1.2 | all-reduce | flops 2 | bytes 16 | tf_op jit(solution)/shard_map/psum | solution.py:103
  649.6 1.9 multiply_reduce_fusion
  651.6 41.4 %psum.23 = f32[]{:T(128)} all-reduce(f32[]{:T(128)} %get-tuple-element.28), channel_id=1, replica_groups=mesh['det'=8,'tm'=4] {'det','tm'}, use_global_device_ids=true, to_apply=%region_11.12 | all-reduce | flops 1 | bytes 8 | tf_op jit(solution)/shard_map/psum | solution.py:107
  (155 shorter events, 23.1 us)
Async XLA Ops:
  0.6 1.1 copy-start
  0.6 21.5 %copy-start.2 = (f32[3,128,256]{2,1,0:T(8,128)S(1)}, f32[3,128,256]{2,1,0:T(8,128)}, u32[]{:S(2)}) copy-start(f32[3,128,256]{2,1,0:T(8,128)} %param.10) | copy-start | bytes 1179652
  4.5 27.6 %copy-start.12 = (s32[256,1]{0,1:T(1,128)}, s32[256,1]{0,1:T(1,128)S(1)}, u32[]{:S(2)}) copy-start(s32[256,1]{0,1:T(1,128)S(1)} %compare_select_fusion.2) | copy-start | bytes 3076
  21.6 0.6 copy-start.10
  28.5 2.9 copy-start.8
  28.5 51.6 %all-to-all-start.1 = ((f32[3,512,256]{2,0,1:T(4,128)}), f32[3,512,256]{2,0,1:T(4,128)S(1)}, u32[]{:S(2)}, u32[]{:S(2)}) async-start(f32[3,512,256]{2,0,1:T(4,128)} %copy.112), calls=%async_computation.1 | async-start | bytes 4194304 | tf_op jit(solution)/shard_map/all_to_all | solution.py:74
  81.9 90.8 %copy-start.5 = (s32[16384]{0:T(1024)S(1)}, s32[16384]{0:T(1024)}, u32[]{:S(2)}) copy-start(s32[16384]{0:T(1024)} %broadcast_clamp_fusion) | copy-start | bytes 196612
  263.3 90.6 %copy-start.6 = (f32[4,4096]{1,0:T(4,128)S(1)}, f32[4,4096]{1,0:T(4,128)}, u32[]{:S(2)}) copy-start(f32[4,4096]{1,0:T(4,128)} %param.12) | copy-start | bytes 196612
  263.3 94.4 %copy-start.7 = (s32[1,1,4,4096]{3,1,2,0:T(1,128)S(1)}, s32[1,1,4,4096]{3,1,2,0:T(1,128)}, u32[]{:S(2)}) copy-start(s32[1,1,4,4096]{3,1,2,0:T(1,128)} %copy.127) | copy-start | bytes 196612
  263.4 94.5 %copy-start.9 = (bf16[4,8192]{1,0:T(4,128)(2,1)S(1)}, bf16[4,8192]{1,0:T(4,128)(2,1)}, u32[]{:S(2)}) copy-start(bf16[4,8192]{1,0:T(4,128)(2,1)} %param.13) | copy-start | bytes 196612
  354.5 40.2 %collective-permute-start = (bf16[4,4096]{1,0:T(4,128)(2,1)S(1)}, bf16[4,4096]{1,0:T(4,128)(2,1)S(1)}, u32[]{:S(2)}, u32[]{:S(2)}) collective-permute-start(bf16[4,4096]{1,0:T(4,128)(2,1)S(1)} %add_convert_fusion), channel_id=1, source_target_pairs={{0,1},{1,2},{2,3},{4,5},{5,6},{6,7},{8,9},{9,10},{10,11},{12,13},{... | collective-permute-start | bytes 98312 | tf_op jit(solution)/shard_map/ppermute | solution.py:12
  356.0 38.7 %collective-permute-start.1 = (bf16[4,4096]{1,0:T(4,128)(2,1)S(1)}, bf16[4,4096]{1,0:T(4,128)(2,1)S(1)}, u32[]{:S(2)}, u32[]{:S(2)}) collective-permute-start(bf16[4,4096]{1,0:T(4,128)(2,1)S(1)} %add_convert_fusion), channel_id=1, source_target_pairs={{1,0},{2,1},{3,2},{5,4},{6,5},{7,6},{9,8},{10,9},{11,10},{13,12},{... | collective-permute-start | bytes 98312 | tf_op jit(solution)/shard_map/ppermute | solution.py:15
  394.7 3.4 slice-start
  508.1 19.6 %copy-start.13 = (s32[256,1]{0,1:T(1,128)S(1)}, s32[256,1]{0,1:T(1,128)}, u32[]{:S(2)}) copy-start(s32[256,1]{0,1:T(1,128)} %copy-done.12) | copy-start | bytes 3076
  551.6 6.9 copy-start.3
  551.6 55.5 %all-to-all-start.2 = ((f32[3,512,256]{2,0,1:T(4,128)}), f32[3,512,256]{2,0,1:T(4,128)S(1)}, u32[]{:S(2)}, u32[]{:S(2)}) async-start(f32[3,512,256]{2,0,1:T(4,128)} %scatter_fusion), calls=%async_computation.2 | async-start | bytes 4194304 | tf_op jit(solution)/shard_map/all_to_all | solution.py:98
  558.3 48.8 %copy-start.11 = (s32[512]{0:T(512)S(1)}, s32[512]{0:T(512)}, u32[]{:S(2)}) copy-start(s32[512]{0:T(512)} %copy-done.10) | copy-start | bytes 6148
  562.0 133.2 %copy-start.4 = (f32[3,128,256]{1,2,0:T(8,128)S(1)}, f32[3,128,256]{1,2,0:T(8,128)}, u32[]{:S(2)}) copy-start(f32[3,128,256]{1,2,0:T(8,128)} %copy.119) | copy-start | bytes 1179652
  694.3 2.8 copy-start.1
where the time goes:
time: 706 us; the launch traced here: 697 us
  local copies, waits for them, and re-layouts  381 us (54%)
  other arithmetic  107 us (15%)
  blocking collectives  94.1 us (13%)
  waiting for transfers between devices  92.4 us (13%)
  starting transfers between devices  12.8 us (2%)
    scatter-add x1, other arithmetic, body(): jnp.zeros((3, per_device * pixels), jnp.float32).at[:, address.reshape(-1)]  101 us
    gather x2, local copies, waits for them, and re-layouts, body(): local_map[0][address] + cosine * local_map[1][address]  90.8 us
    gather x2, local copies, waits for them, and re-layouts, body(): local_map[1][address]  90.6 us
    gather x2, local copies, waits for them, and re-layouts, body(): local_map[2][address]  90.6 us
    all_to_all x1, waiting for transfers between devices, body(): lax.all_to_all(answer, ('det', 'tm'), split_axis=1, concat_axis=1, tiled=...  47.3 us
    all_to_all x1, waiting for transfers between devices, body(): lax.all_to_all(outgoing, ('det', 'tm'), split_axis=1, concat_axis=1, tile...  45.1 us
    psum x1, blocking collectives, body(): norm_new = lax.psum(jnp.sum(r_next * r_next), ('det', 'tm'))  41.4 us
    psum x1, blocking collectives, body(): norm_old = lax.psum(jnp.sum(r_map * r_map), ('det', 'tm'))  38.4 us
  transfers between devices with their start and end apart: 4, of which 2 were waited for; matrix products, arithmetic and copies ran while one was open for 6% of the time, Pallas kernels for 0%

commit v1 on v0

--- a/solution.py
+++ b/solution.py
@@ -95,7 +95,15 @@
         .at[:, send_place, :]
         .set(partial_value.reshape(3, per_device, pixels))
     )
-    returned = lax.all_to_all(outgoing, ("det", "tm"), split_axis=1, concat_axis=1, tiled=True)
+    returned = jnp.concatenate(
+        lax.all_to_all(
+            jnp.stack(jnp.split(outgoing, lax.axis_size(("det", "tm")), axis=1)),
+            ("det", "tm"),
+            0,
+            0,
+        ),
+        axis=1,
+    )
     selector = (asked_slots[:, None] == jnp.arange(blocks_here, dtype=jnp.int32)[None, :]).astype(
         jnp.float32
     )

time: 706 us -> 676 us (0.958)
  local copies, waits for them, and re-layouts: 381 us -> 363 us
  waiting for transfers between devices: 92.4 us -> 82.6 us
    scatter x1, local copies, waits for them, and re-layouts: 24 us -> 6.93 us  [body(): outgoing = jnp.zeros((3, slot_count, pixels), jnp.float32).at[:, send_pla...]
    all_to_all x1, waiting for transfers between devices: 45.1 us -> 35.3 us  [body(): lax.all_to_all(jnp.stack(jnp.split(outgoing, lax.axis_size(('det', 'tm'))...]
    unnamed x107 -> x136, local copies, waits for them, and re-layouts: 27.3 us -> 26.4 us
where the time goes in v1:
time: 676 us; the launch traced here: 668 us
  local copies, waits for them, and re-layouts  363 us (54%)
  other arithmetic  106 us (16%)
  blocking collectives  94 us (14%)
  waiting for transfers between devices  82.6 us (12%)
  starting transfers between devices  12.9 us (2%)
    scatter-add x1, other arithmetic, body(): jnp.zeros((3, per_device * pixels), jnp.float32).at[:, address.reshape(-1)]  101 us
    gather x2, local copies, waits for them, and re-layouts, body(): local_map[0][address] + cosine * local_map[1][address]  90.8 us
    gather x2, local copies, waits for them, and re-layouts, body(): local_map[1][address]  90.6 us
    gather x2, local copies, waits for them, and re-layouts, body(): local_map[2][address]  90.6 us
    all_to_all x1, waiting for transfers between devices, body(): lax.all_to_all(answer, ('det', 'tm'), split_axis=1, concat_axis=1, tiled=...  47.3 us
    psum x1, blocking collectives, body(): norm_new = lax.psum(jnp.sum(r_next * r_next), ('det', 'tm'))  41.6 us
    psum x1, blocking collectives, body(): norm_old = lax.psum(jnp.sum(r_map * r_map), ('det', 'tm'))  38.1 us
    all_to_all x1, waiting for transfers between devices, body(): lax.all_to_all(jnp.stack(jnp.split(outgoing, lax.axis_size(('det', 'tm'))...  35.3 us
  transfers between devices with their start and end apart: 4, of which 2 were waited for; matrix products, arithmetic and copies ran while one was open for 6% of the time, Pallas kernels for 0%

profile of v1, /device:TPU:0, one launch (start us, length us, event | category | flops | bytes accessed | tf_op | source)
XLA Modules:
  0.0 668.2 jit_solution(6447239565400551168)
XLA Ops:
  1.8 1.7 gather_fusion
  6.0 14.2 %all_to_all.22 = s32[32,16,1]{1,2,0:T(1,128)S(1)} all-to-all(s32[32,16,1]{1,2,0:T(1,128)S(1)} %bitcast.565), channel_id=1, replica_groups=mesh['det'=8,'tm'=4] {'det','tm'}, dimensions={0} | all-to-all | bytes 4096 | tf_op jit(solution)/shard_map/all_to_all | solution.py:71
  22.2 3.7 gather_fusion.1
  26.0 2.4 copy.113
  28.5 2.9 all-to-all-start.1
  32.7 47.3 %all-to-all-done.1 = f32[3,512,256]{2,0,1:T(4,128)S(1)} async-done(((f32[3,512,256]{2,0,1:T(4,128)}), f32[3,512,256]{2,0,1:T(4,128)S(1)}, u32[]{:S(2)}, u32[]{:S(2)}) %all-to-all-start.1) | async-done | bytes 1572896 | tf_op jit(solution)/shard_map/all_to_all | solution.py:74
  81.9 90.8 %gather_fusion.3 = f32[16384]{0:T(1024)S(1)} fusion(f32[65536]{0:T(1024)S(1)} %bitcast.486, s32[16384]{0:T(1024)} %broadcast_clamp_fusion), kind=kCustom, calls=%fused_computation.3 | custom fusion | bytes 196608 | tf_op jit(solution)/shard_map/gather | solution.py:83
  172.7 90.5 %gather_fusion.4 = f32[16384]{0:T(1024)S(1)} fusion(f32[65536]{0:T(1024)S(1)} %bitcast.485, s32[16384]{0:T(1024)S(1)} %copy-done.4), kind=kCustom, calls=%fused_computation.4 | custom fusion | bytes 196608 | tf_op jit(solution)/shard_map/gather | solution.py:83
  263.4 90.5 %gather_fusion.5 = f32[16384]{0:T(1024)S(1)} fusion(f32[65536]{0:T(1024)S(1)} %bitcast.484, s32[16384]{0:T(1024)S(1)} %copy-done.4), kind=kCustom, calls=%fused_computation.5 | custom fusion | bytes 196608 | tf_op jit(solution)/shard_map/gather | solution.py:83
  356.0 1.8 collective-permute-start.1
  357.9 3.9 tile.14
  361.7 18.0 %reshape.397 = bf16[4260352]{0:T(1024)(128)(2,1)} reshape(bf16[4,128,8321]{2,1,0:T(8,128)(2,1)} %tile.14) | data formatting | bytes 17041408
  379.7 15.0 %tile.15 = bf16[4,1065088]{1,0:T(4,128)(2,1)} reshape(bf16[4260352]{0:T(1024)(128)(2,1)} %reshape.397) | data formatting | bytes 17041408 | tf_op jit(solution)/shard_map/while/body/eval_jaxpr/vmap()/tile | solution.py:28
  396.2 1.9 slice-done
  398.1 3.0 fusion.12
  402.1 5.2 copy.115
  407.3 100.8 %scatter_custom_fusion.1 = f32[3,65536]{0,1:T(8,128)} fusion(s32[16384]{0:T(1024)S(1)} %bitcast.564, f32[16384,3]{1,0:T(8,128)} %copy.115, f32[]{:T(128)} %constant.81.clone.1), kind=kCustom, calls=%fused_computation.9 | custom fusion | flops 49152 | bytes 786944 | tf_op jit(solution)/shard_map/scatter-add | solution.py:91
  508.1 17.9 %copy.116 = f32[3,256,256]{2,0,1:T(4,128)S(1)} copy(f32[3,256,256]{0,2,1:T(8,128)} %bitcast.487) | data formatting | bytes 1572864 | tf_op jit(solution)/shard_map/reshape | solution.py:96
  526.3 6.9 %scatter_fusion = f32[3,512,256]{2,0,1:T(4,128)S(1)} fusion(f32[3,512,256]{2,0,1:T(4,128)S(1)} %broadcast_in_dim.31, s32[256]{0:T(256)S(1)} %bitcast.569, f32[256,3,256]{2,1,0:T(4,128)S(1)} %bitcast.555), kind=kCustom, calls=%fused_computation.8 | custom fusion | bytes 2360320 | tf_op jit(solution)/shard_map/scatter | solution.py:96
  535.5 6.7 %all-to-all-start.2 = ((f32[32,3,16,256]{3,2,1,0:T(8,128)}), f32[32,3,16,256]{3,2,1,0:T(8,128)S(1)}, u32[]{:S(2)}, u32[]{:S(2)}) async-start(f32[32,3,16,256]{3,2,1,0:T(8,128)} %copy.117), calls=%async_computation.2 | async-start | bytes 3145728 | tf_op jit(solution)/shard_map/all_to_all | solution.py:99
  544.4 35.3 %all-to-all-done.2 = f32[32,3,16,256]{3,2,1,0:T(8,128)S(1)} async-done(((f32[32,3,16,256]{3,2,1,0:T(8,128)}), f32[32,3,16,256]{3,2,1,0:T(8,128)S(1)}, u32[]{:S(2)}, u32[]{:S(2)}) %all-to-all-start.2) | async-done | bytes 1572896 | tf_op jit(solution)/shard_map/all_to_all | solution.py:99
  579.9 2.1 multiply_reduce_fusion.1
  582.0 38.1 %all-reduce.1 = (f32[]{:T(128)}, f32[]{:T(128)}) all-reduce(f32[]{:T(128)} %multiply_reduce_fusion.2, f32[]{:T(128)} %get-tuple-element.41), channel_id=1, replica_groups=mesh['det'=8,'tm'=4] {'det','tm'}, use_global_device_ids=true, to_apply=%region_1.2 | all-reduce | flops 2 | bytes 16 | tf_op jit(solution)/shard_map/psum | solution.py:111
  622.1 41.6 %psum.23 = f32[]{:T(128)} all-reduce(f32[]{:T(128)} %get-tuple-element.28), channel_id=1, replica_groups=mesh['det'=8,'tm'=4] {'det','tm'}, use_global_device_ids=true, to_apply=%region_11.12 | all-reduce | flops 1 | bytes 8 | tf_op jit(solution)/shard_map/psum | solution.py:115
  (187 shorter events, 21.5 us)
Async XLA Ops:
  0.6 1.1 copy-start
  0.6 21.5 %copy-start.2 = (f32[3,128,256]{2,1,0:T(8,128)S(1)}, f32[3,128,256]{2,1,0:T(8,128)}, u32[]{:S(2)}) copy-start(f32[3,128,256]{2,1,0:T(8,128)} %param.10) | copy-start | bytes 1179652
  4.5 27.6 %copy-start.11 = (s32[256,1]{0,1:T(1,128)}, s32[256,1]{0,1:T(1,128)S(1)}, u32[]{:S(2)}) copy-start(s32[256,1]{0,1:T(1,128)S(1)} %compare_select_fusion.2) | copy-start | bytes 3076
  21.6 0.6 copy-start.9
  28.5 2.9 copy-start.7
  28.5 51.6 %all-to-all-start.1 = ((f32[3,512,256]{2,0,1:T(4,128)}), f32[3,512,256]{2,0,1:T(4,128)S(1)}, u32[]{:S(2)}, u32[]{:S(2)}) async-start(f32[3,512,256]{2,0,1:T(4,128)} %copy.113), calls=%async_computation.1 | async-start | bytes 4194304 | tf_op jit(solution)/shard_map/all_to_all | solution.py:74
  81.9 90.8 %copy-start.4 = (s32[16384]{0:T(1024)S(1)}, s32[16384]{0:T(1024)}, u32[]{:S(2)}) copy-start(s32[16384]{0:T(1024)} %broadcast_clamp_fusion) | copy-start | bytes 196612
  263.3 90.6 %copy-start.5 = (f32[4,4096]{1,0:T(4,128)S(1)}, f32[4,4096]{1,0:T(4,128)}, u32[]{:S(2)}) copy-start(f32[4,4096]{1,0:T(4,128)} %param.12) | copy-start | bytes 196612
  263.3 94.4 %copy-start.6 = (s32[1,1,4,4096]{3,1,2,0:T(1,128)S(1)}, s32[1,1,4,4096]{3,1,2,0:T(1,128)}, u32[]{:S(2)}) copy-start(s32[1,1,4,4096]{3,1,2,0:T(1,128)} %copy.131) | copy-start | bytes 196612
  263.3 94.5 %copy-start.8 = (bf16[4,8192]{1,0:T(4,128)(2,1)S(1)}, bf16[4,8192]{1,0:T(4,128)(2,1)}, u32[]{:S(2)}) copy-start(bf16[4,8192]{1,0:T(4,128)(2,1)} %param.13) | copy-start | bytes 196612
  354.4 40.2 %collective-permute-start = (bf16[4,4096]{1,0:T(4,128)(2,1)S(1)}, bf16[4,4096]{1,0:T(4,128)(2,1)S(1)}, u32[]{:S(2)}, u32[]{:S(2)}) collective-permute-start(bf16[4,4096]{1,0:T(4,128)(2,1)S(1)} %add_convert_fusion), channel_id=1, source_target_pairs={{0,1},{1,2},{2,3},{4,5},{5,6},{6,7},{8,9},{9,10},{10,11},{12,13},{... | collective-permute-start | bytes 98312 | tf_op jit(solution)/shard_map/ppermute | solution.py:12
  356.0 38.7 %collective-permute-start.1 = (bf16[4,4096]{1,0:T(4,128)(2,1)S(1)}, bf16[4,4096]{1,0:T(4,128)(2,1)S(1)}, u32[]{:S(2)}, u32[]{:S(2)}) collective-permute-start(bf16[4,4096]{1,0:T(4,128)(2,1)S(1)} %add_convert_fusion), channel_id=1, source_target_pairs={{1,0},{2,1},{3,2},{5,4},{6,5},{7,6},{9,8},{10,9},{11,10},{13,12},{... | collective-permute-start | bytes 98312 | tf_op jit(solution)/shard_map/ppermute | solution.py:15
  394.7 3.4 slice-start
  508.1 18.2 %copy-start.12 = (s32[256,1]{0,1:T(1,128)S(1)}, s32[256,1]{0,1:T(1,128)}, u32[]{:S(2)}) copy-start(s32[256,1]{0,1:T(1,128)} %copy-done.11) | copy-start | bytes 3076
  535.5 6.9 %copy-start.3 = (f32[3,128,256]{2,1,0:T(8,128)S(1)}, f32[3,128,256]{2,1,0:T(8,128)}, u32[]{:S(2)}) copy-start(f32[3,128,256]{2,1,0:T(8,128)} %param.9) | copy-start | bytes 1179652
  535.5 44.2 %all-to-all-start.2 = ((f32[32,3,16,256]{3,2,1,0:T(8,128)}), f32[32,3,16,256]{3,2,1,0:T(8,128)S(1)}, u32[]{:S(2)}, u32[]{:S(2)}) async-start(f32[32,3,16,256]{3,2,1,0:T(8,128)} %copy.117), calls=%async_computation.2 | async-start | bytes 3145728 | tf_op jit(solution)/shard_map/all_to_all | solution.py:99
  542.5 37.3 %copy-start.10 = (s32[512]{0:T(512)S(1)}, s32[512]{0:T(512)}, u32[]{:S(2)}) copy-start(s32[512]{0:T(512)} %copy-done.9) | copy-start | bytes 6148
  665.1 2.8 copy-start.1
